TPU v7x, 256 devices: a whole 4x4x8 slice. The times are simulated.
256 devices in a mesh: variant: 8 (over x, core), mesh: 32 (over z, y).
Axes of the slice: x: 4, y: 4, z: 8, core: 2. Of those that a mesh axis runs over, the one named last changes fastest.
Arguments:
- snapshots: float32 [8, 64, 524288], P('variant', None, 'mesh'), may hold values from -12 to 12, as said below
- ref_index: int32 [1], replicated, may hold values from 0 to 7
- weight_codes: int32 [8], replicated, may hold values from 1 to 16
Outputs:
- new_basis: float32 [64, 524288], P(None, 'mesh')
Inputs may be any that keep to these rules, and one draw needn't show every extreme that they name: `snapshots`: each variant's snapshot matrix has full rank 64, and the principal angles between any two variants' spans have tangents below 0.8.
All inputs are finite; a program needn't handle non-finite values.
Results may differ from a plain program's by a relative error of at most 0.0001.
Values sent between devices are 32-bit elements; how exact they have to be, the bound alone decides.
A program may use at most 64 MiB of HBM per device.

v0:
```python
import math
import jax
import jax.numpy as jnp
from jax import lax
from jax.sharding import Mesh
from jax.sharding import PartitionSpec as P

VARIANT = ("variant_0", "variant_1")
highest = lax.Precision.HIGHEST
atan_coeffs = [(-1.0) ** k / (2 * k + 1) for k in range(24)]
cos_coeffs = [(-1.0) ** k / math.factorial(2 * k) for k in range(24)]
sin_coeffs = [(-1.0) ** k / math.factorial(2 * k + 1) for k in range(24)]


def from_everyone(x, axis):
    count = lax.axis_size(axis)
    return lax.all_to_all(jnp.broadcast_to(x[None], (count, *x.shape)), axis, 0, 0, tiled=True)


def of_everyone(x, axis):
    everything = from_everyone(x, axis)
    return jnp.sum(everything, axis=0)


def spread(x, axes, root):
    x = jnp.where(lax.axis_index(axes) == root, x, jnp.zeros_like(x))
    for axis in axes:
        x = lax.psum(x, axis)
    return x


def product(left, right):
    return jnp.dot(left, right, precision=highest, preferred_element_type=jnp.float32)


def series(matrix, coeffs):
    eye = jnp.eye(matrix.shape[0], dtype=jnp.float32)
    total = coeffs[-1] * eye
    for coeff in reversed(coeffs[:-1]):
        total = coeff * eye + product(matrix, total)
    return total


def inverse(matrix):
    factor = jnp.linalg.cholesky(product(matrix.T, matrix))
    return jax.scipy.linalg.cho_solve((factor, True), matrix.T)


def on_device(snapshots, ref_index, weight_codes):
    own_snap = snapshots[0]
    root = ref_index[0]
    codes = weight_codes.astype(jnp.float32)
    weight = codes[lax.axis_index(VARIANT)] / jnp.sum(codes)
    eye = jnp.eye(own_snap.shape[0], dtype=jnp.float32)
    scale = jnp.float32(math.sqrt(own_snap.shape[1] * lax.axis_size("mesh")))
    gram_own = of_everyone(product(own_snap, own_snap.T), "mesh")
    lower_own = jnp.linalg.cholesky(gram_own)
    base_own = jax.scipy.linalg.solve_triangular(lower_own, own_snap, lower=True)
    base_ref = spread(base_own, VARIANT, root)
    correlation = of_everyone(product(base_ref, base_own.T), "mesh")
    minv = inverse(correlation)
    tangent = product(minv.T, base_own) - base_ref
    tangent_gram = product(minv.T, minv) - eye
    term = weight * product(series(tangent_gram, atan_coeffs), tangent)
    blended = lax.psum(term, VARIANT)
    energy = of_everyone(product(blended, blended.T), "mesh")
    mixed = product(series(energy, cos_coeffs), base_ref) + product(
        series(energy, sin_coeffs), blended
    )
    return mixed * scale


def solution(mesh):
    finer = Mesh(mesh.devices.reshape(4, 2, mesh.shape["mesh"]), ("variant_0", "variant_1", "mesh"))
    placed = (P(VARIANT, None, "mesh"), P(), P())
    return jax.shard_map(
        on_device, mesh=finer, in_specs=placed, out_specs=P(None, "mesh"), check_vma=False
    )
```

profile of v0, /device:TPU:7, one launch (start us, length us, event | category | flops | bytes accessed | tf_op | source)
XLA Modules:
  0.0 408.7 jit_solution(8007824990110213597)
XLA Ops:
  6.5 6.9 %fusion.3 = f32[64,64]{1,0:T(8,128)S(1)} fusion(f32[1,64,16384]{2,1,0:T(8,128)} %param.4), kind=kOutput, calls=%fused_computation.6 | convolution fusion | flops 805306368 | bytes 4210688 | tf_op jit(solution)/shard_map/dot_general | solution.py:33
  13.6 1.4 reshape.19
  15.0 11.2 %all-to-all-start = ((f32[32,1,4096]{2,1,0:T(1,128)}), f32[32,1,4096]{2,1,0:T(1,128)S(1)}, u32[]{:S(2)}, u32[]{:S(2)}) async-start(f32[32,1,4096]{2,1,0:T(1,128)} %reshape.19), calls=%async_computation | async-start | bytes 1048576 | tf_op jit(solution)/shard_map/all_to_all | solution.py:17
  26.3 0.3 all-reduce.4.cloned.1.call-start
  27.3 15.3 %all-to-all-done = f32[32,1,4096]{2,1,0:T(1,128)S(1)} async-done(((f32[32,1,4096]{2,1,0:T(1,128)}), f32[32,1,4096]{2,1,0:T(1,128)S(1)}, u32[]{:S(2)}, u32[]{:S(2)}) %all-to-all-start) | async-done | bytes 524320 | tf_op jit(solution)/shard_map/all_to_all | solution.py:17
  42.5 0.5 broadcast.157
  43.1 1.9 reduce.4
  44.9 0.4 reshape.20
  45.5 5.8 %cholesky.44 = f32[64,64]{1,0:T(8,128)S(1)} custom-call(f32[64,64]{1,0:T(8,128)S(1)} %fusion.15), custom_call_target="Cholesky" | custom-call | tf_op jit(solution)/shard_map/jit(cholesky)/cholesky | solution.py:57
  51.4 0.6 compare_reduce_fusion.1
  52.1 0.7 fusion.7
  52.7 4.9 %custom-call.13 = f32[1,64,64]{1,2,0:T(8,128)S(1)} custom-call(f32[1,64,64]{2,1,0:T(8,128)S(1)} %fusion.7), custom_call_target="InvertDiagBlocksLowerTriangular" | custom-call | tf_op jit(solution)/shard_map/jit(_solve_triangular)/triangular_solve | solution.py:58
  57.6 9.3 %broadcast_select_fusion = (f32[64,16384]{1,0:T(8,128)}, f32[64,16384]{1,0:T(8,128)}) fusion(pred[]{:T(512)S(6)} %eq.142, f32[1,64,16384]{2,1,0:T(8,128)} %param.4, f32[1,64,64]{1,2,0:T(8,128)S(1)} %custom-call.13), kind=kOutput, calls=%fused_computation.8 | convolution fusion | flops 806354944 | bytes 12599297 | tf_op jit(solution)/shard_map/jit(_solve_triangular)/triangular_solve | solution.py:58
  67.0 94.0 %all-reduce.4.cloned.1.call-done = f32[64,16384]{1,0:T(8,128)} async-done(((f32[64,16384]{1,0:T(8,128)}), f32[64,16384]{1,0:T(8,128)}) %all-reduce.4.cloned.1.call-update) | async-done | bytes 4194320 | tf_op jit(solution)/shard_map/psum | solution.py:28
  161.0 44.4 %all-reduce.6.cloned.1.call-done = f32[64,16384]{1,0:T(8,128)} async-done(((f32[64,16384]{1,0:T(8,128)}), f32[64,16384]{1,0:T(8,128)}) %all-reduce.6.cloned.1.call-update) | async-done | bytes 4194320 | tf_op jit(solution)/shard_map/psum | solution.py:28
  205.4 6.9 %fusion.35 = f32[64,64]{1,0:T(8,128)S(1)} fusion(f32[64,16384]{1,0:T(8,128)} %all-reduce.6.cloned.1.call-done, f32[64,16384]{1,0:T(8,128)} %get-tuple-element.7), kind=kOutput, calls=%fused_computation.114 | convolution fusion | flops 805306368 | bytes 8404992 | tf_op jit(solution)/shard_map/dot_general | solution.py:33
  212.5 1.4 reshape.21
  213.9 9.6 %all-to-all-start.1 = ((f32[32,1,4096]{2,1,0:T(1,128)}), f32[32,1,4096]{2,1,0:T(1,128)S(1)}, u32[]{:S(2)}, u32[]{:S(2)}) async-start(f32[32,1,4096]{2,1,0:T(1,128)} %reshape.21), calls=%async_computation.1 | async-start | bytes 1048576 | tf_op jit(solution)/shard_map/all_to_all | solution.py:17
  223.6 0.6 dynamic_slice.3
  224.1 0.6 convert_reduce_fusion
  226.0 14.2 %all-to-all-done.1 = f32[32,1,4096]{2,1,0:T(1,128)S(1)} async-done(((f32[32,1,4096]{2,1,0:T(1,128)}), f32[32,1,4096]{2,1,0:T(1,128)S(1)}, u32[]{:S(2)}, u32[]{:S(2)}) %all-to-all-start.1) | async-done | bytes 524320 | tf_op jit(solution)/shard_map/all_to_all | solution.py:17
  240.2 1.9 reduce.5
  242.0 0.4 reshape.22
  242.5 0.2 fusion.36
  242.9 5.8 %cholesky.55 = f32[64,64]{1,0:T(8,128)S(1)} custom-call(f32[64,64]{1,0:T(8,128)S(1)} %fusion.13), custom_call_target="Cholesky" | custom-call | tf_op jit(solution)/shard_map/jit(cholesky)/cholesky | solution.py:45
  248.8 0.6 compare_reduce_fusion
  249.4 0.7 fusion.8
  250.1 4.9 %custom-call.14 = f32[1,64,64]{1,2,0:T(8,128)S(1)} custom-call(f32[1,64,64]{2,1,0:T(8,128)S(1)} %fusion.8), custom_call_target="InvertDiagBlocksLowerTriangular" | custom-call | tf_op jit(solution)/shard_map/jit(_cho_solve)/triangular_solve | solution.py:46
  255.0 0.2 fusion.11
  255.4 0.2 convolution_subtract_fusion.1
  255.6 0.2 convolution_add_fusion.62
  256.0 0.2 convolution_add_fusion.60
  256.1 0.2 convolution_add_fusion.59
  256.8 0.2 convolution_add_fusion.55
  257.5 0.2 convolution_add_fusion.51
  259.5 7.2 %convolution_subtract_fusion = f32[64,16384]{1,0:T(8,128)S(1)} fusion(f32[64,16384]{1,0:T(8,128)} %all-reduce.6.cloned.1.call-done, f32[64,64]{1,0:T(8,128)S(1)} %fusion.9, f32[64,16384]{1,0:T(8,128)} %get-tuple-element.7), kind=kOutput, calls=%fused_computation.3 | convolution fusion | flops 806354944 | bytes 12599296 | tf_op jit(solution)/shard_map/dot_general | solution.py:33
  266.7 5.4 %convolution_multiply_fusion = f32[64,16384]{1,0:T(8,128)} fusion(f32[64,64]{1,0:T(8,128)S(1)} %convolution_add_fusion.40, f32[64,16384]{1,0:T(8,128)S(1)} %convolution_subtract_fusion, f32[]{:T(128)S(6)} %div.9), kind=kOutput, calls=%fused_computation.2 | convolution fusion | flops 806354944 | bytes 8404996 | tf_op jit(solution)/shard_map/dot_general | solution.py:33
  272.1 74.9 %all-reduce.8.cloned.1.call-done = f32[64,16384]{1,0:T(8,128)} async-done(((f32[64,16384]{1,0:T(8,128)}), f32[64,16384]{1,0:T(8,128)}) %all-reduce.8.cloned.1.call-update) | async-done | bytes 4194320 | tf_op jit(solution)/shard_map/psum | solution.py:65
  347.0 6.9 %fusion.37 = f32[64,64]{1,0:T(8,128)S(1)} fusion(f32[64,16384]{1,0:T(8,128)} %all-reduce.8.cloned.1.call-done), kind=kOutput, calls=%fused_computation.116 | convolution fusion | flops 805306368 | bytes 4210688 | tf_op jit(solution)/shard_map/dot_general | solution.py:33
  354.0 0.7 reshape.23
  354.7 26.7 %all_to_all.15 = f32[32,1,4096]{2,1,0:T(1,128)S(1)} all-to-all(f32[32,1,4096]{2,1,0:T(1,128)S(1)} %reshape.23), channel_id=1, replica_groups=mesh['variant_0'=4,'variant_1'=2,'mesh'=32] {'mesh'}, dimensions={0} | all-to-all | bytes 1048576 | tf_op jit(solution)/shard_map/all_to_all | solution.py:17
  381.4 1.9 reduce.6
  383.2 0.4 reshape.24
  383.7 0.2 fusion.5
  384.4 0.2 convolution_add_fusion.19
  384.6 0.2 convolution_add_fusion.38
  390.9 5.6 %fusion.40 = f32[64,16384]{1,0:T(8,128)S(1)} fusion(f32[64,64]{1,0:T(8,128)S(1)} %convolution_add_fusion.20, f32[64,16384]{1,0:T(8,128)} %all-reduce.6.cloned.1.call-done), kind=kOutput, calls=%fused_computation.119 | convolution fusion | flops 805306368 | bytes 8404992 | tf_op jit(solution)/shard_map/dot_general | solution.py:33
  396.5 5.4 %fusion = f32[64,16384]{1,0:T(8,128)} fusion(f32[64,16384]{1,0:T(8,128)S(1)} %fusion.40, f32[64,64]{1,0:T(8,128)S(1)} %convolution_add_fusion.1, f32[64,16384]{1,0:T(8,128)S(1)} %copy-done), kind=kOutput, calls=%fused_computation.1 | convolution fusion | flops 807403520 | bytes 12599296 | tf_op jit(solution)/shard_map/dot_general | solution.py:33
  (80 shorter events, 10.4 us)
Async XLA Ops:
  15.0 27.5 %all-to-all-start = ((f32[32,1,4096]{2,1,0:T(1,128)}), f32[32,1,4096]{2,1,0:T(1,128)S(1)}, u32[]{:S(2)}, u32[]{:S(2)}) async-start(f32[32,1,4096]{2,1,0:T(1,128)} %reshape.19), calls=%async_computation | async-start | bytes 1048576 | tf_op jit(solution)/shard_map/all_to_all | solution.py:17
  26.3 134.7 %all-reduce.4.cloned.1.call-start = ((), (), s32[]{:S(2)}) async-start(), calls=%async_computation.3 | async-start | bytes 8388608 | tf_op jit(solution)/shard_map/psum | solution.py:28
  66.9 138.5 %all-reduce.6.cloned.1.call-start = ((), (), s32[]{:S(2)}) async-start(), calls=%async_computation.4 | async-start | bytes 8388608 | tf_op jit(solution)/shard_map/psum | solution.py:28
  205.4 18.2 %copy-start.1 = (s32[8]{0:T(128)S(1)}, s32[8]{0:T(128)}, u32[]{:S(2)}) copy-start(s32[8]{0:T(128)} %param.6) | copy-start | bytes 100
  213.9 26.2 %all-to-all-start.1 = ((f32[32,1,4096]{2,1,0:T(1,128)}), f32[32,1,4096]{2,1,0:T(1,128)S(1)}, u32[]{:S(2)}, u32[]{:S(2)}) async-start(f32[32,1,4096]{2,1,0:T(1,128)} %reshape.21), calls=%async_computation.1 | async-start | bytes 1048576 | tf_op jit(solution)/shard_map/all_to_all | solution.py:17
  223.5 123.5 %all-reduce.8.cloned.1.call-start = ((), (), s32[]{:S(2)}) async-start(), calls=%async_computation.5 | async-start | bytes 8388608 | tf_op jit(solution)/shard_map/psum | solution.py:65
  390.9 5.6 %copy-start = (f32[64,16384]{1,0:T(8,128)S(1)}, f32[64,16384]{1,0:T(8,128)}, u32[]{:S(2)}) copy-start(f32[64,16384]{1,0:T(8,128)} %all-reduce.8.cloned.1.call-done) | copy-start | bytes 12582916
Sparse Core Ops, SparseCore 0:
  67.1 93.8 all-reduce.3
  163.9 41.4 all-reduce.5
  272.2 74.6 all-reduce.7
where the time goes:
time: 413 us; the launch traced here: 409 us
  waiting for transfers between devices  243 us (59%)
  matrix products  65.1 us (16%)
  other arithmetic  30.6 us (7%)
  blocking collectives  26.7 us (6%)
  starting transfers between devices  21.2 us (5%)
  between operations  16 us (4%)
  local copies, waits for them, and re-layouts  6.37 us (2%)
    psum x2, waiting for transfers between devices, spread(): x = lax.psum(x, axis)  138 us
    psum x1, waiting for transfers between devices, on_device(): blended = lax.psum(term, VARIANT)  74.9 us
    dot_general x74, matrix products, product(): jnp.dot(left, right, precision=highest, preferred_element_type=jnp.float32)  55.4 us
    all_to_all x2, waiting for transfers between devices, from_everyone(): lax.all_to_all(jnp.broadcast_to(x[None], (count, *x.shape)), axis, 0, 0,...  29.4 us
    all_to_all x1, blocking collectives, from_everyone(): lax.all_to_all(jnp.broadcast_to(x[None], (count, *x.shape)), axis, 0, 0,...  26.7 us
    all_to_all x2, starting transfers between devices, from_everyone(): lax.all_to_all(jnp.broadcast_to(x[None], (count, *x.shape)), axis, 0, 0,...  20.8 us
    another operation x1, matrix products, on_device(): jax.scipy.linalg.solve_triangular(lower_own, own_snap, lower=True)  9.3 us
  transfers between devices with their start and end apart: 5, of which 5 were waited for; matrix products, arithmetic and copies ran while one was open for 0% of the time, Pallas kernels for 0%

commit v1 on v0

--- a/solution.py
+++ b/solution.py
@@ -62,7 +62,7 @@
     tangent = product(minv.T, base_own) - base_ref
     tangent_gram = product(minv.T, minv) - eye
     term = weight * product(series(tangent_gram, atan_coeffs), tangent)
-    blended = lax.psum(term, VARIANT)
+    blended = lax.psum(lax.psum(term, "variant_0"), "variant_1")
     energy = of_everyone(product(blended, blended.T), "mesh")
     mixed = product(series(energy, cos_coeffs), base_ref) + product(
         series(energy, sin_coeffs), blended

time: 413 us -> 477 us (1.15)
  waiting for transfers between devices: 243 us -> 305 us
    psum x1 -> x2, waiting for transfers between devices: 74.9 us -> 138 us  [on_device(): blended = lax.psum(lax.psum(term, 'variant_0'), 'variant_1')]
  transfers between devices with their start and end apart: 5 -> 6, of which waited for: 5 -> 6; matrix products, arithmetic and copies ran while one was open for 0% -> 0% of each run, Pallas kernels for 0% -> 0%
where the time goes in v1:
time: 477 us; the launch traced here: 471 us
  waiting for transfers between devices  305 us (64%)
  matrix products  64.9 us (14%)
  other arithmetic  30.6 us (6%)
  blocking collectives  26 us (5%)
  starting transfers between devices  21.6 us (5%)
  between operations  16 us (3%)
  local copies, waits for them, and re-layouts  6.37 us (1%)
    psum x2, waiting for transfers between devices, spread(): x = lax.psum(x, axis)  138 us
    psum x2, waiting for transfers between devices, on_device(): blended = lax.psum(lax.psum(term, 'variant_0'), 'variant_1')  138 us
    dot_general x74, matrix products, product(): jnp.dot(left, right, precision=highest, preferred_element_type=jnp.float32)  55.2 us
    all_to_all x2, waiting for transfers between devices, from_everyone(): lax.all_to_all(jnp.broadcast_to(x[None], (count, *x.shape)), axis, 0, 0,...  29.3 us
    all_to_all x1, blocking collectives, from_everyone(): lax.all_to_all(jnp.broadcast_to(x[None], (count, *x.shape)), axis, 0, 0,...  26 us
    all_to_all x2, starting transfers between devices, from_everyone(): lax.all_to_all(jnp.broadcast_to(x[None], (count, *x.shape)), axis, 0, 0,...  20.8 us
  transfers between devices with their start and end apart: 6, of which 6 were waited for; matrix products, arithmetic and copies ran while one was open for 0% of the time, Pallas kernels for 0%

profile of v1, /device:TPU:7, one launch (start us, length us, event | category | flops | bytes accessed | tf_op | source)
XLA Modules:
  0.0 470.9 jit_solution(15399729933870020874)
XLA Ops:
  6.5 6.9 %fusion.3 = f32[64,64]{1,0:T(8,128)S(1)} fusion(f32[1,64,16384]{2,1,0:T(8,128)} %param.4), kind=kOutput, calls=%fused_computation.6 | convolution fusion | flops 805306368 | bytes 4210688 | tf_op jit(solution)/shard_map/dot_general | solution.py:33
  13.6 1.4 reshape.19
  15.0 11.2 %all-to-all-start = ((f32[32,1,4096]{2,1,0:T(1,128)}), f32[32,1,4096]{2,1,0:T(1,128)S(1)}, u32[]{:S(2)}, u32[]{:S(2)}) async-start(f32[32,1,4096]{2,1,0:T(1,128)} %reshape.19), calls=%async_computation | async-start | bytes 1048576 | tf_op jit(solution)/shard_map/all_to_all | solution.py:17
  26.3 0.5 all-reduce.5.cloned.1.call-start
  27.4 15.1 %all-to-all-done = f32[32,1,4096]{2,1,0:T(1,128)S(1)} async-done(((f32[32,1,4096]{2,1,0:T(1,128)}), f32[32,1,4096]{2,1,0:T(1,128)S(1)}, u32[]{:S(2)}, u32[]{:S(2)}) %all-to-all-start) | async-done | bytes 524320 | tf_op jit(solution)/shard_map/all_to_all | solution.py:17
  42.5 0.5 broadcast.157
  43.1 1.9 reduce.4
  44.9 0.4 reshape.20
  45.5 5.8 %cholesky.44 = f32[64,64]{1,0:T(8,128)S(1)} custom-call(f32[64,64]{1,0:T(8,128)S(1)} %fusion.15), custom_call_target="Cholesky" | custom-call | tf_op jit(solution)/shard_map/jit(cholesky)/cholesky | solution.py:57
  51.4 0.6 compare_reduce_fusion.1
  52.1 0.7 fusion.7
  52.7 4.9 %custom-call.13 = f32[1,64,64]{1,2,0:T(8,128)S(1)} custom-call(f32[1,64,64]{2,1,0:T(8,128)S(1)} %fusion.7), custom_call_target="InvertDiagBlocksLowerTriangular" | custom-call | tf_op jit(solution)/shard_map/jit(_solve_triangular)/triangular_solve | solution.py:58
  57.6 9.3 %broadcast_select_fusion = (f32[64,16384]{1,0:T(8,128)}, f32[64,16384]{1,0:T(8,128)}) fusion(pred[]{:T(512)S(6)} %eq.142, f32[1,64,16384]{2,1,0:T(8,128)} %param.4, f32[1,64,64]{1,2,0:T(8,128)S(1)} %custom-call.13), kind=kOutput, calls=%fused_computation.8 | convolution fusion | flops 806354944 | bytes 12599297 | tf_op jit(solution)/shard_map/jit(_solve_triangular)/triangular_solve | solution.py:58
  67.0 94.0 %all-reduce.5.cloned.1.call-done = f32[64,16384]{1,0:T(8,128)} async-done(((f32[64,16384]{1,0:T(8,128)}), f32[64,16384]{1,0:T(8,128)}) %all-reduce.5.cloned.1.call-update) | async-done | bytes 4194320 | tf_op jit(solution)/shard_map/psum | solution.py:28
  161.0 44.4 %all-reduce.7.cloned.1.call-done = f32[64,16384]{1,0:T(8,128)} async-done(((f32[64,16384]{1,0:T(8,128)}), f32[64,16384]{1,0:T(8,128)}) %all-reduce.7.cloned.1.call-update) | async-done | bytes 4194320 | tf_op jit(solution)/shard_map/psum | solution.py:28
  205.4 6.9 %fusion.35 = f32[64,64]{1,0:T(8,128)S(1)} fusion(f32[64,16384]{1,0:T(8,128)} %all-reduce.7.cloned.1.call-done, f32[64,16384]{1,0:T(8,128)} %get-tuple-element.7), kind=kOutput, calls=%fused_computation.114 | convolution fusion | flops 805306368 | bytes 8404992 | tf_op jit(solution)/shard_map/dot_general | solution.py:33
  212.5 1.4 reshape.21
  213.9 9.6 %all-to-all-start.1 = ((f32[32,1,4096]{2,1,0:T(1,128)}), f32[32,1,4096]{2,1,0:T(1,128)S(1)}, u32[]{:S(2)}, u32[]{:S(2)}) async-start(f32[32,1,4096]{2,1,0:T(1,128)} %reshape.21), calls=%async_computation.1 | async-start | bytes 1048576 | tf_op jit(solution)/shard_map/all_to_all | solution.py:17
  223.6 0.6 dynamic_slice.3
  224.1 0.6 convert_reduce_fusion
  226.0 14.2 %all-to-all-done.1 = f32[32,1,4096]{2,1,0:T(1,128)S(1)} async-done(((f32[32,1,4096]{2,1,0:T(1,128)}), f32[32,1,4096]{2,1,0:T(1,128)S(1)}, u32[]{:S(2)}, u32[]{:S(2)}) %all-to-all-start.1) | async-done | bytes 524320 | tf_op jit(solution)/shard_map/all_to_all | solution.py:17
  240.2 1.9 reduce.5
  242.0 0.4 reshape.22
  242.5 0.2 fusion.36
  242.9 5.8 %cholesky.55 = f32[64,64]{1,0:T(8,128)S(1)} custom-call(f32[64,64]{1,0:T(8,128)S(1)} %fusion.13), custom_call_target="Cholesky" | custom-call | tf_op jit(solution)/shard_map/jit(cholesky)/cholesky | solution.py:45
  248.8 0.6 compare_reduce_fusion
  249.4 0.7 fusion.8
  250.1 4.9 %custom-call.14 = f32[1,64,64]{1,2,0:T(8,128)S(1)} custom-call(f32[1,64,64]{2,1,0:T(8,128)S(1)} %fusion.8), custom_call_target="InvertDiagBlocksLowerTriangular" | custom-call | tf_op jit(solution)/shard_map/jit(_cho_solve)/triangular_solve | solution.py:46
  255.0 0.2 fusion.11
  255.4 0.2 convolution_subtract_fusion.1
  255.6 0.2 convolution_add_fusion.62
  256.0 0.2 convolution_add_fusion.60
  256.1 0.2 convolution_add_fusion.59
  259.5 7.2 %convolution_subtract_fusion = f32[64,16384]{1,0:T(8,128)S(1)} fusion(f32[64,16384]{1,0:T(8,128)} %all-reduce.7.cloned.1.call-done, f32[64,64]{1,0:T(8,128)S(1)} %fusion.9, f32[64,16384]{1,0:T(8,128)} %get-tuple-element.7), kind=kOutput, calls=%fused_computation.3 | convolution fusion | flops 806354944 | bytes 12599296 | tf_op jit(solution)/shard_map/dot_general | solution.py:33
  266.7 5.2 %convolution_multiply_fusion = f32[64,16384]{1,0:T(8,128)} fusion(f32[64,64]{1,0:T(8,128)S(1)} %convolution_add_fusion.40, f32[64,16384]{1,0:T(8,128)S(1)} %convolution_subtract_fusion, f32[]{:T(128)S(6)} %div.9), kind=kOutput, calls=%fused_computation.2 | convolution fusion | flops 806354944 | bytes 8404996 | tf_op jit(solution)/shard_map/dot_general | solution.py:33
  272.0 0.3 all-reduce.11.cloned.1.call-start
  272.2 93.4 %all-reduce.9.cloned.1.call-done = f32[64,16384]{1,0:T(8,128)} async-done(((f32[64,16384]{1,0:T(8,128)}), f32[64,16384]{1,0:T(8,128)}) %all-reduce.9.cloned.1.call-update) | async-done | bytes 4194320 | tf_op jit(solution)/shard_map/psum | solution.py:65
  365.6 44.3 %all-reduce.11.cloned.1.call-done = f32[64,16384]{1,0:T(8,128)} async-done(((f32[64,16384]{1,0:T(8,128)}), f32[64,16384]{1,0:T(8,128)}) %all-reduce.11.cloned.1.call-update) | async-done | bytes 4194320 | tf_op jit(solution)/shard_map/psum | solution.py:65
  409.9 6.9 %fusion.37 = f32[64,64]{1,0:T(8,128)S(1)} fusion(f32[64,16384]{1,0:T(8,128)} %all-reduce.11.cloned.1.call-done), kind=kOutput, calls=%fused_computation.116 | convolution fusion | flops 805306368 | bytes 4210688 | tf_op jit(solution)/shard_map/dot_general | solution.py:33
  417.0 0.7 reshape.23
  417.6 26.0 %all_to_all.15 = f32[32,1,4096]{2,1,0:T(1,128)S(1)} all-to-all(f32[32,1,4096]{2,1,0:T(1,128)S(1)} %reshape.23), channel_id=1, replica_groups=mesh['variant_0'=4,'variant_1'=2,'mesh'=32] {'mesh'}, dimensions={0} | all-to-all | bytes 1048576 | tf_op jit(solution)/shard_map/all_to_all | solution.py:17
  443.6 1.9 reduce.6
  445.5 0.4 reshape.24
  446.0 0.2 fusion.5
  446.7 0.2 convolution_add_fusion.19
  446.9 0.2 convolution_add_fusion.38
  453.2 5.6 %fusion.40 = f32[64,16384]{1,0:T(8,128)S(1)} fusion(f32[64,64]{1,0:T(8,128)S(1)} %convolution_add_fusion.20, f32[64,16384]{1,0:T(8,128)} %all-reduce.7.cloned.1.call-done), kind=kOutput, calls=%fused_computation.119 | convolution fusion | flops 805306368 | bytes 8404992 | tf_op jit(solution)/shard_map/dot_general | solution.py:33
  458.8 5.4 %fusion = f32[64,16384]{1,0:T(8,128)} fusion(f32[64,16384]{1,0:T(8,128)S(1)} %fusion.40, f32[64,64]{1,0:T(8,128)S(1)} %convolution_add_fusion.1, f32[64,16384]{1,0:T(8,128)S(1)} %copy-done), kind=kOutput, calls=%fused_computation.1 | convolution fusion | flops 807403520 | bytes 12599296 | tf_op jit(solution)/shard_map/dot_general | solution.py:33
  (83 shorter events, 10.7 us)
Async XLA Ops:
  15.0 27.5 %all-to-all-start = ((f32[32,1,4096]{2,1,0:T(1,128)}), f32[32,1,4096]{2,1,0:T(1,128)S(1)}, u32[]{:S(2)}, u32[]{:S(2)}) async-start(f32[32,1,4096]{2,1,0:T(1,128)} %reshape.19), calls=%async_computation | async-start | bytes 1048576 | tf_op jit(solution)/shard_map/all_to_all | solution.py:17
  26.3 134.7 %all-reduce.5.cloned.1.call-start = ((), (), s32[]{:S(2)}) async-start(), calls=%async_computation.3 | async-start | bytes 8388608 | tf_op jit(solution)/shard_map/psum | solution.py:28
  66.9 138.5 %all-reduce.7.cloned.1.call-start = ((), (), s32[]{:S(2)}) async-start(), calls=%async_computation.4 | async-start | bytes 8388608 | tf_op jit(solution)/shard_map/psum | solution.py:28
  205.4 18.2 %copy-start.1 = (s32[8]{0:T(128)S(1)}, s32[8]{0:T(128)}, u32[]{:S(2)}) copy-start(s32[8]{0:T(128)} %param.6) | copy-start | bytes 100
  213.9 26.2 %all-to-all-start.1 = ((f32[32,1,4096]{2,1,0:T(1,128)}), f32[32,1,4096]{2,1,0:T(1,128)S(1)}, u32[]{:S(2)}, u32[]{:S(2)}) async-start(f32[32,1,4096]{2,1,0:T(1,128)} %reshape.21), calls=%async_computation.1 | async-start | bytes 1048576 | tf_op jit(solution)/shard_map/all_to_all | solution.py:17
  223.5 142.1 %all-reduce.9.cloned.1.call-start = ((), (), s32[]{:S(2)}) async-start(), calls=%async_computation.5 | async-start | bytes 8388608 | tf_op jit(solution)/shard_map/psum | solution.py:65
  272.0 137.9 %all-reduce.11.cloned.1.call-start = ((), (), s32[]{:S(2)}) async-start(), calls=%async_computation.6 | async-start | bytes 8388608 | tf_op jit(solution)/shard_map/psum | solution.py:65
  453.2 5.6 %copy-start = (f32[64,16384]{1,0:T(8,128)S(1)}, f32[64,16384]{1,0:T(8,128)}, u32[]{:S(2)}) copy-start(f32[64,16384]{1,0:T(8,128)} %all-reduce.11.cloned.1.call-done) | copy-start | bytes 12582916
Sparse Core Ops, SparseCore 0:
  67.1 93.8 all-reduce.4
  163.9 41.4 all-reduce.6
  272.1 93.4 all-reduce.8
  368.4 41.4 all-reduce.10
